TPU v7x, 256 devices: a whole 4x4x8 slice. The times are simulated.
256 devices in a mesh: variant: 8 (over x, core), mesh: 32 (over z, y).
Axes of the slice: x: 4, y: 4, z: 8, core: 2. Of those that a mesh axis runs over, the one named last changes fastest.
Arguments:
- snapshots: float32 [8, 64, 524288], P('variant', None, 'mesh'), may hold values from -12 to 12, as said below
- ref_index: int32 [1], replicated, may hold values from 0 to 7
- weight_codes: int32 [8], replicated, may hold values from 1 to 16
Outputs:
- new_basis: float32 [64, 524288], P(None, 'mesh')
Inputs may be any that keep to these rules, and one draw needn't show every extreme that they name: `snapshots`: each variant's snapshot matrix has full rank 64, and the principal angles between any two variants' spans have tangents below 0.8.
All inputs are finite; a program needn't handle non-finite values.
Results may differ from a plain program's by a relative error of at most 0.0001.
Values sent between devices are 32-bit elements; how exact they have to be, the bound alone decides.
A program may use at most 64 MiB of HBM per device.

v0:
```python
import math
import jax
import jax.numpy as jnp
from jax import lax
from jax.sharding import Mesh
from jax.sharding import PartitionSpec as P

VARIANT = ("variant_0", "variant_1")
highest = lax.Precision.HIGHEST
atan_coeffs = [(-1.0) ** k / (2 * k + 1) for k in range(24)]
cos_coeffs = [(-1.0) ** k / math.factorial(2 * k) for k in range(24)]
sin_coeffs = [(-1.0) ** k / math.factorial(2 * k + 1) for k in range(24)]


def from_everyone(x, axis):
    count = lax.axis_size(axis)
    return lax.all_to_all(jnp.broadcast_to(x[None], (count, *x.shape)), axis, 0, 0, tiled=True)


def of_everyone(x, axis):
    everything = from_everyone(x, axis)
    return jnp.sum(everything, axis=0)


def spread(x, axes, root):
    x = jnp.where(lax.axis_index(axes) == root, x, jnp.zeros_like(x))
    for axis in axes:
        x = lax.psum(x, axis)
    return x


def product(left, right):
    return jnp.dot(left, right, precision=highest, preferred_element_type=jnp.float32)


def series(matrix, coeffs):
    eye = jnp.eye(matrix.shape[0], dtype=jnp.float32)
    total = coeffs[-1] * eye
    for coeff in reversed(coeffs[:-1]):
        total = coeff * eye + product(matrix, total)
    return total


def inverse(matrix):
    factor = jnp.linalg.cholesky(product(matrix.T, matrix))
    return jax.scipy.linalg.cho_solve((factor, True), matrix.T)


def on_device(snapshots, ref_index, weight_codes):
    own_snap = snapshots[0]
    root = ref_index[0]
    codes = weight_codes.astype(jnp.float32)
    weight = codes[lax.axis_index(VARIANT)] / jnp.sum(codes)
    eye = jnp.eye(own_snap.shape[0], dtype=jnp.float32)
    scale = jnp.float32(math.sqrt(own_snap.shape[1] * lax.axis_size("mesh")))
    gram_own = of_everyone(product(own_snap, own_snap.T), "mesh")
    lower_own = jnp.linalg.cholesky(gram_own)
    base_own = jax.scipy.linalg.solve_triangular(lower_own, own_snap, lower=True)
    base_ref = spread(base_own, VARIANT, root)
    correlation = of_everyone(product(base_ref, base_own.T), "mesh")
    minv = inverse(correlation)
    tangent = product(minv.T, base_own) - base_ref
    tangent_gram = product(minv.T, minv) - eye
    term = weight * product(series(tangent_gram, atan_coeffs), tangent)
    blended = lax.psum(term, VARIANT)
    energy = of_everyone(product(blended, blended.T), "mesh")
    mixed = product(series(energy, cos_coeffs), base_ref) + product(
        series(energy, sin_coeffs), blended
    )
    return mixed * scale


def solution(mesh):
    finer = Mesh(mesh.devices.reshape(4, 2, mesh.shape["mesh"]), ("variant_0", "variant_1", "mesh"))
    placed = (P(VARIANT, None, "mesh"), P(), P())
    return jax.shard_map(
        on_device, mesh=finer, in_specs=placed, out_specs=P(None, "mesh"), check_vma=False
    )
```

profile of v0, /device:TPU:7, one launch (start us, length us, event | category | flops | bytes accessed | tf_op | source)
XLA Modules:
  0.0 408.7 jit_solution(8007824990110213597)
XLA Ops:
  6.5 6.9 %fusion.3 = f32[64,64]{1,0:T(8,128)S(1)} fusion(f32[1,64,16384]{2,1,0:T(8,128)} %param.4), kind=kOutput, calls=%fused_computation.6 | convolution fusion | flops 805306368 | bytes 4210688 | tf_op jit(solution)/shard_map/dot_general | solution.py:33
  13.6 1.4 reshape.19
  15.0 11.2 %all-to-all-start = ((f32[32,1,4096]{2,1,0:T(1,128)}), f32[32,1,4096]{2,1,0:T(1,128)S(1)}, u32[]{:S(2)}, u32[]{:S(2)}) async-start(f32[32,1,4096]{2,1,0:T(1,128)} %reshape.19), calls=%async_computation | async-start | bytes 1048576 | tf_op jit(solution)/shard_map/all_to_all | solution.py:17
  27.3 15.3 %all-to-all-done = f32[32,1,4096]{2,1,0:T(1,128)S(1)} async-done(((f32[32,1,4096]{2,1,0:T(1,128)}), f32[32,1,4096]{2,1,0:T(1,128)S(1)}, u32[]{:S(2)}, u32[]{:S(2)}) %all-to-all-start) | async-done | bytes 524320 | tf_op jit(solution)/shard_map/all_to_all | solution.py:17
  43.1 1.9 reduce.4
  45.5 5.8 %cholesky.44 = f32[64,64]{1,0:T(8,128)S(1)} custom-call(f32[64,64]{1,0:T(8,128)S(1)} %fusion.15), custom_call_target="Cholesky" | custom-call | tf_op jit(solution)/shard_map/jit(cholesky)/cholesky | solution.py:57
  52.7 4.9 %custom-call.13 = f32[1,64,64]{1,2,0:T(8,128)S(1)} custom-call(f32[1,64,64]{2,1,0:T(8,128)S(1)} %fusion.7), custom_call_target="InvertDiagBlocksLowerTriangular" | custom-call | tf_op jit(solution)/shard_map/jit(_solve_triangular)/triangular_solve | solution.py:58
  57.6 9.3 %broadcast_select_fusion = (f32[64,16384]{1,0:T(8,128)}, f32[64,16384]{1,0:T(8,128)}) fusion(pred[]{:T(512)S(6)} %eq.142, f32[1,64,16384]{2,1,0:T(8,128)} %param.4, f32[1,64,64]{1,2,0:T(8,128)S(1)} %custom-call.13), kind=kOutput, calls=%fused_computation.8 | convolution fusion | flops 806354944 | bytes 12599297 | tf_op jit(solution)/shard_map/jit(_solve_triangular)/triangular_solve | solution.py:58
  67.0 94.0 %all-reduce.4.cloned.1.call-done = f32[64,16384]{1,0:T(8,128)} async-done(((f32[64,16384]{1,0:T(8,128)}), f32[64,16384]{1,0:T(8,128)}) %all-reduce.4.cloned.1.call-update) | async-done | bytes 4194320 | tf_op jit(solution)/shard_map/psum | solution.py:28
  161.0 44.4 %all-reduce.6.cloned.1.call-done = f32[64,16384]{1,0:T(8,128)} async-done(((f32[64,16384]{1,0:T(8,128)}), f32[64,16384]{1,0:T(8,128)}) %all-reduce.6.cloned.1.call-update) | async-done | bytes 4194320 | tf_op jit(solution)/shard_map/psum | solution.py:28
  205.4 6.9 %fusion.35 = f32[64,64]{1,0:T(8,128)S(1)} fusion(f32[64,16384]{1,0:T(8,128)} %all-reduce.6.cloned.1.call-done, f32[64,16384]{1,0:T(8,128)} %get-tuple-element.7), kind=kOutput, calls=%fused_computation.114 | convolution fusion | flops 805306368 | bytes 8404992 | tf_op jit(solution)/shard_map/dot_general | solution.py:33
  213.9 9.6 %all-to-all-start.1 = ((f32[32,1,4096]{2,1,0:T(1,128)}), f32[32,1,4096]{2,1,0:T(1,128)S(1)}, u32[]{:S(2)}, u32[]{:S(2)}) async-start(f32[32,1,4096]{2,1,0:T(1,128)} %reshape.21), calls=%async_computation.1 | async-start | bytes 1048576 | tf_op jit(solution)/shard_map/all_to_all | solution.py:17
  226.0 14.2 %all-to-all-done.1 = f32[32,1,4096]{2,1,0:T(1,128)S(1)} async-done(((f32[32,1,4096]{2,1,0:T(1,128)}), f32[32,1,4096]{2,1,0:T(1,128)S(1)}, u32[]{:S(2)}, u32[]{:S(2)}) %all-to-all-start.1) | async-done | bytes 524320 | tf_op jit(solution)/shard_map/all_to_all | solution.py:17
  240.2 1.9 reduce.5
  242.9 5.8 %cholesky.55 = f32[64,64]{1,0:T(8,128)S(1)} custom-call(f32[64,64]{1,0:T(8,128)S(1)} %fusion.13), custom_call_target="Cholesky" | custom-call | tf_op jit(solution)/shard_map/jit(cholesky)/cholesky | solution.py:45
  250.1 4.9 %custom-call.14 = f32[1,64,64]{1,2,0:T(8,128)S(1)} custom-call(f32[1,64,64]{2,1,0:T(8,128)S(1)} %fusion.8), custom_call_target="InvertDiagBlocksLowerTriangular" | custom-call | tf_op jit(solution)/shard_map/jit(_cho_solve)/triangular_solve | solution.py:46
  259.5 7.2 %convolution_subtract_fusion = f32[64,16384]{1,0:T(8,128)S(1)} fusion(f32[64,16384]{1,0:T(8,128)} %all-reduce.6.cloned.1.call-done, f32[64,64]{1,0:T(8,128)S(1)} %fusion.9, f32[64,16384]{1,0:T(8,128)} %get-tuple-element.7), kind=kOutput, calls=%fused_computation.3 | convolution fusion | flops 806354944 | bytes 12599296 | tf_op jit(solution)/shard_map/dot_general | solution.py:33
  266.7 5.4 %convolution_multiply_fusion = f32[64,16384]{1,0:T(8,128)} fusion(f32[64,64]{1,0:T(8,128)S(1)} %convolution_add_fusion.40, f32[64,16384]{1,0:T(8,128)S(1)} %convolution_subtract_fusion, f32[]{:T(128)S(6)} %div.9), kind=kOutput, calls=%fused_computation.2 | convolution fusion | flops 806354944 | bytes 8404996 | tf_op jit(solution)/shard_map/dot_general | solution.py:33
  272.1 74.9 %all-reduce.8.cloned.1.call-done = f32[64,16384]{1,0:T(8,128)} async-done(((f32[64,16384]{1,0:T(8,128)}), f32[64,16384]{1,0:T(8,128)}) %all-reduce.8.cloned.1.call-update) | async-done | bytes 4194320 | tf_op jit(solution)/shard_map/psum | solution.py:65
  347.0 6.9 %fusion.37 = f32[64,64]{1,0:T(8,128)S(1)} fusion(f32[64,16384]{1,0:T(8,128)} %all-reduce.8.cloned.1.call-done), kind=kOutput, calls=%fused_computation.116 | convolution fusion | flops 805306368 | bytes 4210688 | tf_op jit(solution)/shard_map/dot_general | solution.py:33
  354.7 26.7 %all_to_all.15 = f32[32,1,4096]{2,1,0:T(1,128)S(1)} all-to-all(f32[32,1,4096]{2,1,0:T(1,128)S(1)} %reshape.23), channel_id=1, replica_groups=mesh['variant_0'=4,'variant_1'=2,'mesh'=32] {'mesh'}, dimensions={0} | all-to-all | bytes 1048576 | tf_op jit(solution)/shard_map/all_to_all | solution.py:17
  381.4 1.9 reduce.6
  390.9 5.6 %fusion.40 = f32[64,16384]{1,0:T(8,128)S(1)} fusion(f32[64,64]{1,0:T(8,128)S(1)} %convolution_add_fusion.20, f32[64,16384]{1,0:T(8,128)} %all-reduce.6.cloned.1.call-done), kind=kOutput, calls=%fused_computation.119 | convolution fusion | flops 805306368 | bytes 8404992 | tf_op jit(solution)/shard_map/dot_general | solution.py:33
  396.5 5.4 %fusion = f32[64,16384]{1,0:T(8,128)} fusion(f32[64,16384]{1,0:T(8,128)S(1)} %fusion.40, f32[64,64]{1,0:T(8,128)S(1)} %convolution_add_fusion.1, f32[64,16384]{1,0:T(8,128)S(1)} %copy-done), kind=kOutput, calls=%fused_computation.1 | convolution fusion | flops 807403520 | bytes 12599296 | tf_op jit(solution)/shard_map/dot_general | solution.py:33
  (104 shorter events, 20.4 us)
Async XLA Ops:
  15.0 27.5 %all-to-all-start = ((f32[32,1,4096]{2,1,0:T(1,128)}), f32[32,1,4096]{2,1,0:T(1,128)S(1)}, u32[]{:S(2)}, u32[]{:S(2)}) async-start(f32[32,1,4096]{2,1,0:T(1,128)} %reshape.19), calls=%async_computation | async-start | bytes 1048576 | tf_op jit(solution)/shard_map/all_to_all | solution.py:17
  26.3 134.7 %all-reduce.4.cloned.1.call-start = ((), (), s32[]{:S(2)}) async-start(), calls=%async_computation.3 | async-start | bytes 8388608 | tf_op jit(solution)/shard_map/psum | solution.py:28
  66.9 138.5 %all-reduce.6.cloned.1.call-start = ((), (), s32[]{:S(2)}) async-start(), calls=%async_computation.4 | async-start | bytes 8388608 | tf_op jit(solution)/shard_map/psum | solution.py:28
  205.4 18.2 %copy-start.1 = (s32[8]{0:T(128)S(1)}, s32[8]{0:T(128)}, u32[]{:S(2)}) copy-start(s32[8]{0:T(128)} %param.6) | copy-start | bytes 100
  213.9 26.2 %all-to-all-start.1 = ((f32[32,1,4096]{2,1,0:T(1,128)}), f32[32,1,4096]{2,1,0:T(1,128)S(1)}, u32[]{:S(2)}, u32[]{:S(2)}) async-start(f32[32,1,4096]{2,1,0:T(1,128)} %reshape.21), calls=%async_computation.1 | async-start | bytes 1048576 | tf_op jit(solution)/shard_map/all_to_all | solution.py:17
  223.5 123.5 %all-reduce.8.cloned.1.call-start = ((), (), s32[]{:S(2)}) async-start(), calls=%async_computation.5 | async-start | bytes 8388608 | tf_op jit(solution)/shard_map/psum | solution.py:65
  390.9 5.6 %copy-start = (f32[64,16384]{1,0:T(8,128)S(1)}, f32[64,16384]{1,0:T(8,128)}, u32[]{:S(2)}) copy-start(f32[64,16384]{1,0:T(8,128)} %all-reduce.8.cloned.1.call-done) | copy-start | bytes 12582916
Sparse Core Ops, SparseCore 0:
  67.1 93.8 all-reduce.3
  163.9 41.4 all-reduce.5
  272.2 74.6 all-reduce.7
where the time goes:
time: 413 us; the launch traced here: 409 us
  waiting for transfers between devices  243 us (59%)
  matrix products  65.1 us (16%)
  other arithmetic  30.6 us (7%)
  blocking collectives  26.7 us (6%)
  starting transfers between devices  21.2 us (5%)
  between operations  16 us (4%)
  local copies, waits for them, and re-layouts  6.37 us (2%)
    psum x2, waiting for transfers between devices, spread(): x = lax.psum(x, axis)  138 us
    psum x1, waiting for transfers between devices, on_device(): blended = lax.psum(term, VARIANT)  74.9 us
    dot_general x74, matrix products, product(): jnp.dot(left, right, precision=highest, preferred_element_type=jnp.float32)  55.4 us
    all_to_all x2, waiting for transfers between devices, from_everyone(): lax.all_to_all(jnp.broadcast_to(x[None], (count, *x.shape)), axis, 0, 0,...  29.4 us
    all_to_all x1, blocking collectives, from_everyone(): lax.all_to_all(jnp.broadcast_to(x[None], (count, *x.shape)), axis, 0, 0,...  26.7 us
    all_to_all x2, starting transfers between devices, from_everyone(): lax.all_to_all(jnp.broadcast_to(x[None], (count, *x.shape)), axis, 0, 0,...  20.8 us
    another operation x1, matrix products, on_device(): jax.scipy.linalg.solve_triangular(lower_own, own_snap, lower=True)  9.3 us
  transfers between devices with their start and end apart: 5, of which 5 were waited for; matrix products, arithmetic and copies ran while one was open for 0% of the time, Pallas kernels for 0%

commit v1 on v0

--- a/solution.py
+++ b/solution.py
@@ -25,7 +25,11 @@
 def spread(x, axes, root):
     x = jnp.where(lax.axis_index(axes) == root, x, jnp.zeros_like(x))
     for axis in axes:
-        x = lax.psum(x, axis)
+
+        def pack_the_quarters(panel):
+            return lax.all_gather(panel, axis).sum(axis=0)
+
+        x = pack_the_quarters(x)
     return x
 
 

time: 413 us -> 472 us (1.14)
  waiting for transfers between devices: 243 us -> 285 us
  other arithmetic: 30.6 us -> 46.5 us
    all_gather x0 -> x2, waiting for transfers between devices: none -> 181 us  [pack_the_quarters(): return lax.all_gather(panel, axis).sum(axis=0)]
    psum x2 -> x0, waiting for transfers between devices: 138 us -> none  [spread(): x = lax.psum(x, axis)]
    reduce_sum x0 -> x2, other arithmetic: none -> 15.8 us  [pack_the_quarters(): return lax.all_gather(panel, axis).sum(axis=0)]
where the time goes in v1:
time: 472 us; the launch traced here: 468 us
  waiting for transfers between devices  285 us (60%)
  matrix products  65.2 us (14%)
  other arithmetic  46.5 us (10%)
  blocking collectives  26.7 us (6%)
  starting transfers between devices  21.9 us (5%)
  between operations  16.1 us (3%)
  local copies, waits for them, and re-layouts  6.48 us (1%)
    all_gather x2, waiting for transfers between devices, pack_the_quarters(): return lax.all_gather(panel, axis).sum(axis=0)  181 us
    psum x1, waiting for transfers between devices, on_device(): blended = lax.psum(term, VARIANT)  74.8 us
    dot_general x74, matrix products, product(): jnp.dot(left, right, precision=highest, preferred_element_type=jnp.float32)  55.4 us
    all_to_all x2, waiting for transfers between devices, from_everyone(): lax.all_to_all(jnp.broadcast_to(x[None], (count, *x.shape)), axis, 0, 0,...  29.1 us
    all_to_all x1, blocking collectives, from_everyone(): lax.all_to_all(jnp.broadcast_to(x[None], (count, *x.shape)), axis, 0, 0,...  26.7 us
    all_to_all x2, starting transfers between devices, from_everyone(): lax.all_to_all(jnp.broadcast_to(x[None], (count, *x.shape)), axis, 0, 0,...  20.8 us
    reduce_sum x2, other arithmetic, pack_the_quarters(): return lax.all_gather(panel, axis).sum(axis=0)  15.8 us
  transfers between devices with their start and end apart: 5, of which 5 were waited for; matrix products, arithmetic and copies ran while one was open for 0% of the time, Pallas kernels for 0%

profile of v1, /device:TPU:7, one launch (start us, length us, event | category | flops | bytes accessed | tf_op | source)
XLA Modules:
  0.0 467.7 jit_solution(15681664673907301742)
XLA Ops:
  6.5 6.9 %fusion.3 = f32[64,64]{1,0:T(8,128)S(1)} fusion(f32[1,64,16384]{2,1,0:T(8,128)} %param.4), kind=kOutput, calls=%fused_computation.6 | convolution fusion | flops 805306368 | bytes 4210688 | tf_op jit(solution)/shard_map/dot_general | solution.py:37
  15.0 11.2 %all-to-all-start = ((f32[32,1,4096]{2,1,0:T(1,128)}), f32[32,1,4096]{2,1,0:T(1,128)S(1)}, u32[]{:S(2)}, u32[]{:S(2)}) async-start(f32[32,1,4096]{2,1,0:T(1,128)} %reshape.21), calls=%async_computation | async-start | bytes 1048576 | tf_op jit(solution)/shard_map/all_to_all | solution.py:17
  27.3 15.3 %all-to-all-done = f32[32,1,4096]{2,1,0:T(1,128)S(1)} async-done(((f32[32,1,4096]{2,1,0:T(1,128)}), f32[32,1,4096]{2,1,0:T(1,128)S(1)}, u32[]{:S(2)}, u32[]{:S(2)}) %all-to-all-start) | async-done | bytes 524320 | tf_op jit(solution)/shard_map/all_to_all | solution.py:17
  45.6 5.8 %cholesky.44 = f32[64,64]{1,0:T(8,128)S(1)} custom-call(f32[64,64]{1,0:T(8,128)S(1)} %fusion.15), custom_call_target="Cholesky" | custom-call | tf_op jit(solution)/shard_map/jit(cholesky)/cholesky | solution.py:61
  52.7 4.9 %custom-call.13 = f32[1,64,64]{1,2,0:T(8,128)S(1)} custom-call(f32[1,64,64]{2,1,0:T(8,128)S(1)} %fusion.7), custom_call_target="InvertDiagBlocksLowerTriangular" | custom-call | tf_op jit(solution)/shard_map/jit(_solve_triangular)/triangular_solve | solution.py:62
  57.6 9.3 %broadcast_select_fusion = (f32[64,16384]{1,0:T(8,128)}, f32[64,16384]{1,0:T(8,128)}) fusion(pred[]{:T(512)S(6)} %eq.142, f32[1,64,16384]{2,1,0:T(8,128)} %param.4, f32[1,64,64]{1,2,0:T(8,128)S(1)} %custom-call.13), kind=kOutput, calls=%fused_computation.8 | convolution fusion | flops 806354944 | bytes 12599297 | tf_op jit(solution)/shard_map/jit(_solve_triangular)/triangular_solve | solution.py:62
  67.5 152.3 %all-gather.5.cloned.1.call-done = f32[256,16384]{1,0:T(8,128)} async-done(((f32[64,16384]{1,0:T(8,128)}), f32[256,16384]{1,0:T(8,128)}) %all-gather.5.cloned.1.call-update) | async-done | bytes 16777232 | tf_op jit(solution)/shard_map/all_gather | solution.py:30
  219.8 9.3 %reduce_sum.56 = f32[64,16384]{1,0:T(8,128)} reduce(f32[4,64,16384]{2,1,0:T(8,128)} %bitcast.178, f32[]{:T(128)} %constant.189.clone.1), dimensions={0}, to_apply=%region_4.6 | reduce | flops 3145728 | bytes 20971524 | tf_op jit(solution)/shard_map/reduce_sum | solution.py:30
  229.2 28.5 %all-gather.7.cloned.1.call-done = f32[128,16384]{1,0:T(8,128)} async-done(((f32[64,16384]{1,0:T(8,128)}), f32[128,16384]{1,0:T(8,128)}) %all-gather.7.cloned.1.call-update) | async-done | bytes 8388624 | tf_op jit(solution)/shard_map/all_gather | solution.py:30
  257.7 6.5 %reduce_sum.57 = f32[64,16384]{1,0:T(8,128)} reduce(f32[2,64,16384]{2,1,0:T(8,128)} %bitcast.179, f32[]{:T(128)} %constant.189.clone.1), dimensions={0}, to_apply=%region_5.7 | reduce | flops 1048576 | bytes 12582916 | tf_op jit(solution)/shard_map/reduce_sum | solution.py:30
  264.2 6.9 %fusion.35 = f32[64,64]{1,0:T(8,128)S(1)} fusion(f32[64,16384]{1,0:T(8,128)} %reduce_sum.57, f32[64,16384]{1,0:T(8,128)} %get-tuple-element.7), kind=kOutput, calls=%fused_computation.114 | convolution fusion | flops 805306368 | bytes 8404992 | tf_op jit(solution)/shard_map/dot_general | solution.py:37
  272.7 9.6 %all-to-all-start.1 = ((f32[32,1,4096]{2,1,0:T(1,128)}), f32[32,1,4096]{2,1,0:T(1,128)S(1)}, u32[]{:S(2)}, u32[]{:S(2)}) async-start(f32[32,1,4096]{2,1,0:T(1,128)} %reshape.23), calls=%async_computation.1 | async-start | bytes 1048576 | tf_op jit(solution)/shard_map/all_to_all | solution.py:17
  285.1 13.9 %all-to-all-done.1 = f32[32,1,4096]{2,1,0:T(1,128)S(1)} async-done(((f32[32,1,4096]{2,1,0:T(1,128)}), f32[32,1,4096]{2,1,0:T(1,128)S(1)}, u32[]{:S(2)}, u32[]{:S(2)}) %all-to-all-start.1) | async-done | bytes 524320 | tf_op jit(solution)/shard_map/all_to_all | solution.py:17
  299.0 1.9 reduce.5
  301.7 5.8 %cholesky.55 = f32[64,64]{1,0:T(8,128)S(1)} custom-call(f32[64,64]{1,0:T(8,128)S(1)} %fusion.13), custom_call_target="Cholesky" | custom-call | tf_op jit(solution)/shard_map/jit(cholesky)/cholesky | solution.py:49
  309.0 4.9 %custom-call.14 = f32[1,64,64]{1,2,0:T(8,128)S(1)} custom-call(f32[1,64,64]{2,1,0:T(8,128)S(1)} %fusion.8), custom_call_target="InvertDiagBlocksLowerTriangular" | custom-call | tf_op jit(solution)/shard_map/jit(_cho_solve)/triangular_solve | solution.py:50
  314.3 7.2 %convolution_subtract_fusion = f32[64,16384]{1,0:T(8,128)S(1)} fusion(f32[64,16384]{1,0:T(8,128)} %reduce_sum.57, f32[64,64]{1,0:T(8,128)S(1)} %fusion.9, f32[64,16384]{1,0:T(8,128)} %get-tuple-element.7), kind=kOutput, calls=%fused_computation.3 | convolution fusion | flops 806354944 | bytes 12599296 | tf_op jit(solution)/shard_map/dot_general | solution.py:37
  325.7 5.4 %convolution_multiply_fusion = f32[64,16384]{1,0:T(8,128)} fusion(f32[64,64]{1,0:T(8,128)S(1)} %convolution_add_fusion.40, f32[64,16384]{1,0:T(8,128)S(1)} %convolution_subtract_fusion, f32[]{:T(128)S(6)} %div.9), kind=kOutput, calls=%fused_computation.2 | convolution fusion | flops 806354944 | bytes 8404996 | tf_op jit(solution)/shard_map/dot_general | solution.py:37
  331.1 74.8 %all-reduce.2.cloned.1.call-done = f32[64,16384]{1,0:T(8,128)} async-done(((f32[64,16384]{1,0:T(8,128)}), f32[64,16384]{1,0:T(8,128)}) %all-reduce.2.cloned.1.call-update) | async-done | bytes 4194320 | tf_op jit(solution)/shard_map/psum | solution.py:69
  406.0 6.9 %fusion.37 = f32[64,64]{1,0:T(8,128)S(1)} fusion(f32[64,16384]{1,0:T(8,128)} %all-reduce.2.cloned.1.call-done), kind=kOutput, calls=%fused_computation.116 | convolution fusion | flops 805306368 | bytes 4210688 | tf_op jit(solution)/shard_map/dot_general | solution.py:37
  413.7 26.7 %all_to_all.15 = f32[32,1,4096]{2,1,0:T(1,128)S(1)} all-to-all(f32[32,1,4096]{2,1,0:T(1,128)S(1)} %reshape.25), channel_id=1, replica_groups=mesh['variant_0'=4,'variant_1'=2,'mesh'=32] {'mesh'}, dimensions={0} | all-to-all | bytes 1048576 | tf_op jit(solution)/shard_map/all_to_all | solution.py:17
  440.4 1.9 reduce.6
  446.9 5.6 %fusion.40 = f32[64,16384]{1,0:T(8,128)S(1)} fusion(f32[64,64]{1,0:T(8,128)S(1)} %convolution_add_fusion.20, f32[64,16384]{1,0:T(8,128)} %reduce_sum.57), kind=kOutput, calls=%fused_computation.119 | convolution fusion | flops 805306368 | bytes 8404992 | tf_op jit(solution)/shard_map/dot_general | solution.py:37
  455.5 5.4 %fusion = f32[64,16384]{1,0:T(8,128)} fusion(f32[64,16384]{1,0:T(8,128)S(1)} %fusion.40, f32[64,64]{1,0:T(8,128)S(1)} %convolution_add_fusion.1, f32[64,16384]{1,0:T(8,128)S(1)} %copy-done), kind=kOutput, calls=%fused_computation.1 | convolution fusion | flops 807403520 | bytes 12599296 | tf_op jit(solution)/shard_map/dot_general | solution.py:37
  (106 shorter events, 24.6 us)
Async XLA Ops:
  15.0 27.5 %all-to-all-start = ((f32[32,1,4096]{2,1,0:T(1,128)}), f32[32,1,4096]{2,1,0:T(1,128)S(1)}, u32[]{:S(2)}, u32[]{:S(2)}) async-start(f32[32,1,4096]{2,1,0:T(1,128)} %reshape.21), calls=%async_computation | async-start | bytes 1048576 | tf_op jit(solution)/shard_map/all_to_all | solution.py:17
  26.3 193.6 %all-gather.5.cloned.1.call-start = ((), (), s32[]{:S(2)}) async-start(), calls=%async_computation.4 | async-start | bytes 20971520 | tf_op jit(solution)/shard_map/all_gather | solution.py:30
  67.0 190.8 %all-gather.7.cloned.1.call-start = ((), (), s32[]{:S(2)}) async-start(), calls=%async_computation.5 | async-start | bytes 12582912 | tf_op jit(solution)/shard_map/all_gather | solution.py:30
  264.2 18.3 %copy-start.1 = (s32[8]{0:T(128)S(1)}, s32[8]{0:T(128)}, u32[]{:S(2)}) copy-start(s32[8]{0:T(128)} %param.6) | copy-start | bytes 100
  272.7 26.2 %all-to-all-start.1 = ((f32[32,1,4096]{2,1,0:T(1,128)}), f32[32,1,4096]{2,1,0:T(1,128)S(1)}, u32[]{:S(2)}, u32[]{:S(2)}) async-start(f32[32,1,4096]{2,1,0:T(1,128)} %reshape.23), calls=%async_computation.1 | async-start | bytes 1048576 | tf_op jit(solution)/shard_map/all_to_all | solution.py:17
  282.3 123.6 %all-reduce.2.cloned.1.call-start = ((), (), s32[]{:S(2)}) async-start(), calls=%async_computation.3 | async-start | bytes 8388608 | tf_op jit(solution)/shard_map/psum | solution.py:69
  446.8 8.7 %copy-start = (f32[64,16384]{1,0:T(8,128)S(1)}, f32[64,16384]{1,0:T(8,128)}, u32[]{:S(2)}) copy-start(f32[64,16384]{1,0:T(8,128)} %all-reduce.2.cloned.1.call-done) | copy-start | bytes 12582916
Sparse Core Ops, SparseCore 0:
  67.1 152.7 all-gather.4
  229.3 28.3 all-gather.6
  331.3 74.6 all-reduce.1
